TPU v7x, 32 devices: a whole 2x2x4 slice. The times are simulated.
32 devices in a mesh: seq: 8 (over y, x, core), dp: 4 (over z).
Axes of the slice: x: 2, y: 2, z: 4, core: 2. Of those that a mesh axis runs over, the one named last changes fastest.
Arguments:
- normed_input: bfloat16 [4, 1024, 5376], P('dp', 'seq'), may hold values from -6 to 6
- q_base: bfloat16 [4, 1024, 2048], P('dp', 'seq'), may hold values from -6 to 6
- k_base: bfloat16 [4, 1024, 1024], P('dp', 'seq'), may hold values from -6 to 6
- v_base: bfloat16 [4, 1024, 1024], P('dp', 'seq'), may hold values from -6 to 6
- d_attn: bfloat16 [4, 1024, 2048], P('dp', 'seq'), may hold values from -0.09375 to 0.09375
- lengths: int32 [4], P('dp'), may hold values from 512 to 1024
- a_query: bfloat16 [5376, 16], replicated, may hold values from -0.078125 to 0.078125
- b_query: bfloat16 [16, 2048], replicated, may hold values from -0.8984375 to 0.8984375
- a_key: bfloat16 [5376, 16], replicated, may hold values from -0.078125 to 0.078125
- b_key: bfloat16 [16, 1024], replicated, may hold values from -0.8984375 to 0.8984375
- a_value: bfloat16 [5376, 16], replicated, may hold values from -0.078125 to 0.078125
- b_value: bfloat16 [16, 1024], replicated, may hold values from -0.8984375 to 0.8984375
Outputs:
- attention: bfloat16 [4, 1024, 2048], P('dp', 'seq')
- grad_a_query: float32 [5376, 16], replicated
- grad_b_query: float32 [16, 2048], replicated
- grad_a_key: float32 [5376, 16], replicated
- grad_b_key: float32 [16, 1024], replicated
- grad_a_value: float32 [5376, 16], replicated
- grad_b_value: float32 [16, 1024], replicated
All inputs are finite; a program needn't handle non-finite values.
Results may differ from a plain program's by a relative error of at most 0.006.
The roundings to bfloat16 on the way count: a program that leaves them out, or rounds other values in their place, can miss the bound.
Values may be sent and summed in bfloat16 or wider, within the bound.
A program may use at most 64 MiB of HBM per device.

v0:
```python
import jax
import jax.numpy as jnp
from jax import lax
from jax.sharding import PartitionSpec as P

HD = 128
WINDOW = 384
attn_scale = 168.0 ** (-0.5)
mask_fill = -1e30


def shifted(value, axis, steps):
    count = lax.axis_size(axis)
    leading, last = (max(0, -steps), min(count, count - steps))
    return lax.ppermute(value, axis, [(source, source + steps) for source in range(leading, last)])


def attend(query, keyset, values, d_out, allowed):
    scores = (
        jnp.einsum("qgrd,kgd->grqk", query, keyset, preferred_element_type=jnp.float32) * attn_scale
    )
    scores = jnp.where(allowed[None, None], scores, mask_fill)
    top_score = jnp.max(scores, axis=-1, keepdims=True)
    raw_weight = jnp.exp(scores - top_score)
    probs = raw_weight / jnp.sum(raw_weight, axis=-1, keepdims=True)
    probs_low = probs.astype(jnp.bfloat16)
    output = jnp.einsum("grqk,kgd->qgrd", probs_low, values, preferred_element_type=jnp.float32)
    dprob = jnp.einsum("qgrd,kgd->grqk", d_out, values, preferred_element_type=jnp.float32)
    delta = jnp.sum(probs * dprob, axis=-1, keepdims=True)
    dscore = (probs * (dprob - delta)).astype(jnp.bfloat16)
    d_query = (
        jnp.einsum("grqk,kgd->qgrd", dscore, keyset, preferred_element_type=jnp.float32)
        * attn_scale
    )
    d_key = (
        jnp.einsum("grqk,qgrd->kgd", dscore, query, preferred_element_type=jnp.float32) * attn_scale
    )
    d_value = jnp.einsum("grqk,qgrd->kgd", probs_low, d_out, preferred_element_type=jnp.float32)
    return (output, d_query, d_key, d_value)


def lifted(base, low, b_matrix):
    return (
        base.astype(jnp.float32) + jnp.dot(low, b_matrix, preferred_element_type=jnp.float32)
    ).astype(jnp.bfloat16)


def fetch_blocks(key_own, value_own, low_pair, hop_count):
    earlier = []
    current = (key_own, value_own, low_pair)
    for hop_index in range(1, hop_count + 1):
        current = shifted((current[0], current[1], current[2]), "seq", 1)
        earlier.append(current)
    return earlier


def shards(
    normed_input,
    q_base,
    k_base,
    v_base,
    d_attn,
    lengths,
    a_query,
    b_query,
    a_key,
    b_key,
    a_value,
    b_value,
):
    rows = normed_input[0]
    tok_rows = rows.shape[0]
    hop_count = (WINDOW + tok_rows - 1) // tok_rows
    rank_size = a_query.shape[1]
    shard_index = lax.axis_index("seq")
    length = lengths[0]
    a_joined = jnp.concatenate([a_query, a_key, a_value], 1)
    low_all = jnp.dot(rows, a_joined, preferred_element_type=jnp.float32).astype(jnp.bfloat16)
    low_query = low_all[:, :rank_size]
    low_pair = low_all[:, rank_size:]
    query = lifted(q_base[0], low_query, b_query)
    key_own = lifted(k_base[0], low_pair[:, :rank_size], b_key)
    value_own = lifted(v_base[0], low_pair[:, rank_size:], b_value)
    earlier = fetch_blocks(key_own, value_own, low_pair, hop_count)
    ordered = list(reversed(earlier))
    key_rows = jnp.concatenate([block[0] for block in ordered] + [key_own], 0)
    value_rows = jnp.concatenate([block[1] for block in ordered] + [value_own], 0)
    low_rows = jnp.concatenate([block[2] for block in ordered] + [low_pair], 0)
    key_span = key_rows.shape[0]
    query_pos = shard_index * tok_rows + jnp.arange(tok_rows, dtype=jnp.int32)
    key_pos = shard_index * tok_rows - hop_count * tok_rows + jnp.arange(key_span, dtype=jnp.int32)
    offset = query_pos[:, None] - key_pos[None, :]
    allowed = (
        (key_pos[None, :] >= 0)
        & (offset >= 0)
        & (offset <= WINDOW)
        & ((key_pos[None, :] < length) | (offset == 0))
    )
    live = query_pos < length
    grad_out = d_attn[0]
    d_out = jnp.where(live[:, None], grad_out, jnp.zeros_like(grad_out))
    groups = key_rows.shape[1] // (2 * HD)
    query_grp = query.reshape(tok_rows, groups, 2, 2, HD).transpose(1, 0, 2, 3, 4)
    dout_grp = d_out.reshape(tok_rows, groups, 2, 2, HD).transpose(1, 0, 2, 3, 4)
    key_grp = key_rows.reshape(key_span, groups, 2, HD).transpose(1, 0, 2, 3)
    value_grp = value_rows.reshape(key_span, groups, 2, HD).transpose(1, 0, 2, 3)

    def per_group(packed):
        return attend(packed[0], packed[1], packed[2], packed[3], allowed)

    out_grp, dquery_grp, dkey_grp, dvalue_grp = lax.map(
        per_group, (query_grp, key_grp, value_grp, dout_grp)
    )
    output = out_grp.transpose(1, 0, 2, 3, 4).reshape(tok_rows, -1)
    attention = jnp.where(live[:, None], output, jnp.zeros_like(output)).astype(jnp.bfloat16)
    d_query = dquery_grp.transpose(1, 0, 2, 3, 4).reshape(tok_rows, -1)
    d_key = dkey_grp.transpose(1, 0, 2, 3).reshape(key_span, -1)
    d_value = dvalue_grp.transpose(1, 0, 2, 3).reshape(key_span, -1)
    highest = lax.Precision.HIGHEST
    u_query = jnp.dot(d_query, b_query.astype(jnp.float32).T, precision=highest).astype(
        jnp.bfloat16
    )
    grad_b_query = jnp.dot(low_query.astype(jnp.float32).T, d_query, precision=highest)
    low_keys = low_rows[:, :rank_size].astype(jnp.float32)
    low_values = low_rows[:, rank_size:].astype(jnp.float32)
    grad_b_key = jnp.dot(low_keys.T, d_key, precision=highest)
    grad_b_value = jnp.dot(low_values.T, d_value, precision=highest)
    ukey_all = jnp.dot(d_key, b_key.astype(jnp.float32).T, precision=highest)
    uvalue_all = jnp.dot(d_value, b_value.astype(jnp.float32).T, precision=highest)
    own_start = hop_count * tok_rows
    ukey_sum = ukey_all[own_start:]
    uvalue_sum = uvalue_all[own_start:]
    for hop_index in range(1, hop_count + 1):
        lower = (hop_count - hop_index) * tok_rows
        came = shifted(
            (ukey_all[lower : lower + tok_rows], uvalue_all[lower : lower + tok_rows]),
            "seq",
            -hop_index,
        )
        ukey_sum = ukey_sum + came[0]
        uvalue_sum = uvalue_sum + came[1]
    u_key = ukey_sum.astype(jnp.bfloat16)
    u_value = uvalue_sum.astype(jnp.bfloat16)
    grad_a_query = jnp.einsum("td,tr->dr", rows, u_query, preferred_element_type=jnp.float32)
    grad_a_key = jnp.einsum("td,tr->dr", rows, u_key, preferred_element_type=jnp.float32)
    grad_a_value = jnp.einsum("td,tr->dr", rows, u_value, preferred_element_type=jnp.float32)
    totals = lax.psum(
        (grad_a_query, grad_b_query, grad_a_key, grad_b_key, grad_a_value, grad_b_value),
        ("seq", "dp"),
    )
    return (attention[None], totals[0], totals[1], totals[2], totals[3], totals[4], totals[5])


def solution(mesh):
    return jax.shard_map(
        shards,
        mesh=mesh,
        in_specs=(
            P("dp", "seq", None),
            P("dp", "seq", None),
            P("dp", "seq", None),
            P("dp", "seq", None),
            P("dp", "seq", None),
            P("dp"),
            P(),
            P(),
            P(),
            P(),
            P(),
            P(),
        ),
        out_specs=(P("dp", "seq", None), P(), P(), P(), P(), P(), P()),
        check_vma=False,
    )
```

profile of v0, /device:TPU:0, one launch (start us, length us, event | category | flops | bytes accessed | tf_op | source)
XLA Modules:
  0.0 273.2 jit_solution(176504505119206906)
XLA Ops:
  10.4 3.1 %collective-permute-start.3 = (bf16[128,1024]{1,0:T(8,128)(2,1)S(1)}, bf16[128,1024]{1,0:T(8,128)(2,1)}, u32[]{:S(2)}, u32[]{:S(2)}) collective-permute-start(bf16[128,1024]{1,0:T(8,128)(2,1)S(1)} %fusion.78), channel_id=1, source_target_pairs={{0,4},{4,8},{8,12},{12,16},{16,20},{20,24},{24,28},{1,5},{5,9},{9,... | collective-permute-start | bytes 786440 | tf_op jit(solution)/shard_map/ppermute | solution.py:15
  13.8 4.5 %collective-permute-start = (bf16[128,1024]{1,0:T(8,128)(2,1)S(1)}, bf16[128,1024]{1,0:T(8,128)(2,1)}, u32[]{:S(2)}, u32[]{:S(2)}) collective-permute-start(bf16[128,1024]{1,0:T(8,128)(2,1)S(1)} %fusion.77), channel_id=1, source_target_pairs={{0,4},{4,8},{8,12},{12,16},{16,20},{20,24},{24,28},{1,5},{5,9},{9,... | collective-permute-start | bytes 786440 | tf_op jit(solution)/shard_map/ppermute | solution.py:15
  18.9 1.9 collective-permute-start.9
  22.1 2.9 %collective-permute-start.4 = (bf16[128,1024]{1,0:T(8,128)(2,1)}, bf16[128,1024]{1,0:T(8,128)(2,1)S(1)}, u32[]{:S(2)}, u32[]{:S(2)}) collective-permute-start(bf16[128,1024]{1,0:T(8,128)(2,1)} %collective-permute-done.3), channel_id=1, source_target_pairs={{0,4},{4,8},{8,12},{12,16},{16,20},{20,24},{24,28},{1,5},{5,9},{9,... | collective-permute-start | bytes 786440 | tf_op jit(solution)/shard_map/ppermute | solution.py:15
  25.0 2.6 collective-permute-start.1
  28.5 2.8 %collective-permute-start.10 = (bf16[128,32]{0,1:T(8,128)(2,1)}, bf16[128,32]{0,1:T(8,128)(2,1)S(1)}, u32[]{:S(2)}, u32[]{:S(2)}) collective-permute-start(bf16[128,32]{0,1:T(8,128)(2,1)} %collective-permute-done.9), channel_id=1, source_target_pairs={{0,4},{4,8},{8,12},{12,16},{16,20},{20,24},{24,28},{1,5},{5,9},{9,... | collective-permute-start | bytes 24584 | tf_op jit(solution)/shard_map/ppermute | solution.py:15
  31.3 1.9 collective-permute-start.5
  33.3 1.9 collective-permute-start.11
  35.2 3.9 %collective-permute-start.2 = (bf16[128,1024]{1,0:T(8,128)(2,1)}, bf16[128,1024]{1,0:T(8,128)(2,1)}, u32[]{:S(2)}, u32[]{:S(2)}) collective-permute-start(bf16[128,1024]{1,0:T(8,128)(2,1)} %collective-permute-done.1), channel_id=1, source_target_pairs={{0,4},{4,8},{8,12},{12,16},{16,20},{20,24},{24,28},{1,5},{5,9},{9,... | collective-permute-start | bytes 786440 | tf_op jit(solution)/shard_map/ppermute | solution.py:15
  47.6 47.8 %while.17 = (s32[]{:T(128)}, bf16[4,128,2,2,128]{1,4,3,2,0:T(8,128)(2,1)}, f32[4,128,2,2,128]{1,4,3,2,0:T(8,128)}, f32[4,512,2,128]{1,3,2,0:T(8,128)}, f32[4,512...) while((s32[]{:T(128)}, ...), condition=%wide.region_4.5_spmd.clone, body=%wide.region_0.4_spmd.clone.sunk | while | flops 543098880 | bytes 17327832 | solution.py:111
  51.4 2.1 fusion.172
  54.5 2.5 fusion.173
  63.4 2.1 fusion.172
  66.5 2.5 fusion.173
  75.3 2.1 fusion.172
  78.4 2.5 fusion.173
  87.3 2.1 fusion.172
  90.3 2.5 fusion.173
  95.3 2.5 fusion.118
  109.4 1.9 fusion.104
  115.1 3.3 %collective-permute-done.7 = f32[128,16]{0,1:T(8,128)S(1)} collective-permute-done((f32[128,16]{0,1:T(8,128)S(1)}, f32[128,16]{0,1:T(8,128)S(1)}, u32[]{:S(2)}, u32[]{:S(2)}) %collective-permute-start.7) | collective-permute-done | bytes 8224 | tf_op jit(solution)/shard_map/ppermute | solution.py:15
  118.5 2.5 collective-permute-done.8
  123.2 134.2 %all-reduce.3.cloned.1.call-done = (f32[5376,16]{0,1:T(8,128)}, f32[16,2048]{1,0:T(8,128)}, f32[5376,16]{0,1:T(8,128)}, f32[16,1024]{1,0:T(8,128)}, f32[5376,16]{0,1:T(8,128)}, /*index=5*/f32[16,1024]{1,0:T(8,128)}) async-done(((f32[5376,16]{0,1:T(8,128)}, f32[16,2048]{1,0:T(8,128)}, f32[5376,16]{0,1:T(8,128)}, f32[16,1024]{1,0:T(8,128)}, f32[5376,16]{0,1:T(8,128)}, /*index=5*/f32[16,1024]{1,0:T(8,128)}), ...) | async-done | bytes 1294352 | tf_op jit(solution)/shard_map/psum | solution.py:147
  257.5 1.8 copy.96
  (150 shorter events, 67.6 us)
Async XLA Ops:
  7.2 14.2 %copy-start.7 = (bf16[1,128,2048]{2,1,0:T(8,128)(2,1)S(1)}, bf16[1,128,2048]{2,1,0:T(8,128)(2,1)}, u32[]{:S(2)}) copy-start(bf16[1,128,2048]{2,1,0:T(8,128)(2,1)} %param.18) | copy-start | bytes 1572868
  7.2 14.5 %copy-start.8 = (bf16[1,128,2048]{2,1,0:T(8,128)(2,1)S(1)}, bf16[1,128,2048]{2,1,0:T(8,128)(2,1)}, u32[]{:S(2)}) copy-start(bf16[1,128,2048]{2,1,0:T(8,128)(2,1)} %param.15) | copy-start | bytes 1572868
  7.2 14.5 %copy-start.12 = (bf16[16,2048]{1,0:T(8,128)(2,1)S(1)}, bf16[16,2048]{1,0:T(8,128)(2,1)}, u32[]{:S(2)}) copy-start(bf16[16,2048]{1,0:T(8,128)(2,1)} %param.21) | copy-start | bytes 196612
  7.2 250.2 %all-reduce.3.cloned.1.call-start = ((), (), s32[]{:S(2)}) async-start(), calls=%async_computation | async-start | bytes 2588672 | tf_op jit(solution)/shard_map/psum | solution.py:147
  10.2 18.3 %copy-start.21 = (bf16[128,48]{0,1:T(8,128)(2,1)}, bf16[128,48]{0,1:T(8,128)(2,1)S(1)}, u32[]{:S(2)}) copy-start(bf16[128,48]{0,1:T(8,128)(2,1)S(1)} %fusion.82) | copy-start | bytes 36868
  10.4 11.6 %collective-permute-start.3 = (bf16[128,1024]{1,0:T(8,128)(2,1)S(1)}, bf16[128,1024]{1,0:T(8,128)(2,1)}, u32[]{:S(2)}, u32[]{:S(2)}) collective-permute-start(bf16[128,1024]{1,0:T(8,128)(2,1)S(1)} %fusion.78), channel_id=1, source_target_pairs={{0,4},{4,8},{8,12},{12,16},{16,20},{20,24},{24,28},{1,5},{5,9},{9,... | collective-permute-start | bytes 786440 | tf_op jit(solution)/shard_map/ppermute | solution.py:15
  13.8 26.2 %copy-start.5 = (bf16[128,1024]{1,0:T(8,128)(2,1)}, bf16[128,1024]{1,0:T(8,128)(2,1)S(1)}, u32[]{:S(2)}) copy-start(bf16[128,1024]{1,0:T(8,128)(2,1)S(1)} %fusion.77) | copy-start | bytes 786436
  13.8 11.2 %collective-permute-start = (bf16[128,1024]{1,0:T(8,128)(2,1)S(1)}, bf16[128,1024]{1,0:T(8,128)(2,1)}, u32[]{:S(2)}, u32[]{:S(2)}) collective-permute-start(bf16[128,1024]{1,0:T(8,128)(2,1)S(1)} %fusion.77), channel_id=1, source_target_pairs={{0,4},{4,8},{8,12},{12,16},{16,20},{20,24},{24,28},{1,5},{5,9},{9,... | collective-permute-start | bytes 786440 | tf_op jit(solution)/shard_map/ppermute | solution.py:15
  18.9 9.6 %collective-permute-start.9 = (bf16[128,32]{0,1:T(8,128)(2,1)}, bf16[128,32]{0,1:T(8,128)(2,1)}, u32[]{:S(2)}, u32[]{:S(2)}) collective-permute-start(bf16[128,32]{0,1:T(8,128)(2,1)} %slice.65), channel_id=1, source_target_pairs={{0,4},{4,8},{8,12},{12,16},{16,20},{20,24},{24,28},{1,5},{5,9},{9,... | collective-permute-start | bytes 24584 | tf_op jit(solution)/shard_map/ppermute | solution.py:15
  21.5 11.8 %copy-start.22 = (pred[128]{0:T(512)(128)(4,1)}, pred[128]{0:T(512)(128)(4,1)S(1)}, u32[]{:S(2)}) copy-start(pred[128]{0:T(512)(128)(4,1)S(1)} %broadcast_compare_fusion) | copy-start | bytes 388
  22.1 9.2 %collective-permute-start.4 = (bf16[128,1024]{1,0:T(8,128)(2,1)}, bf16[128,1024]{1,0:T(8,128)(2,1)S(1)}, u32[]{:S(2)}, u32[]{:S(2)}) collective-permute-start(bf16[128,1024]{1,0:T(8,128)(2,1)} %collective-permute-done.3), channel_id=1, source_target_pairs={{0,4},{4,8},{8,12},{12,16},{16,20},{20,24},{24,28},{1,5},{5,9},{9,... | collective-permute-start | bytes 786440 | tf_op jit(solution)/shard_map/ppermute | solution.py:15
  25.0 10.2 %collective-permute-start.1 = (bf16[128,1024]{1,0:T(8,128)(2,1)}, bf16[128,1024]{1,0:T(8,128)(2,1)}, u32[]{:S(2)}, u32[]{:S(2)}) collective-permute-start(bf16[128,1024]{1,0:T(8,128)(2,1)} %collective-permute-done), channel_id=1, source_target_pairs={{0,4},{4,8},{8,12},{12,16},{16,20},{20,24},{24,28},{1,5},{5,9},{9,... | collective-permute-start | bytes 786440 | tf_op jit(solution)/shard_map/ppermute | solution.py:15
  28.5 4.8 %collective-permute-start.10 = (bf16[128,32]{0,1:T(8,128)(2,1)}, bf16[128,32]{0,1:T(8,128)(2,1)S(1)}, u32[]{:S(2)}, u32[]{:S(2)}) collective-permute-start(bf16[128,32]{0,1:T(8,128)(2,1)} %collective-permute-done.9), channel_id=1, source_target_pairs={{0,4},{4,8},{8,12},{12,16},{16,20},{20,24},{24,28},{1,5},{5,9},{9,... | collective-permute-start | bytes 24584 | tf_op jit(solution)/shard_map/ppermute | solution.py:15
  31.3 11.0 %collective-permute-start.5 = (bf16[128,1024]{1,0:T(8,128)(2,1)S(1)}, bf16[128,1024]{1,0:T(8,128)(2,1)S(1)}, u32[]{:S(2)}, u32[]{:S(2)}) collective-permute-start(bf16[128,1024]{1,0:T(8,128)(2,1)S(1)} %collective-permute-done.4), channel_id=1, source_target_pairs={{0,4},{4,8},{8,12},{12,16},{16,20},{20,24},{24,28},{1,5},{5,9},{9,... | collective-permute-start | bytes 786440 | tf_op jit(solution)/shard_map/ppermute | solution.py:15
  33.3 7.7 %collective-permute-start.11 = (bf16[128,32]{0,1:T(8,128)(2,1)S(1)}, bf16[128,32]{0,1:T(8,128)(2,1)S(1)}, u32[]{:S(2)}, u32[]{:S(2)}) collective-permute-start(bf16[128,32]{0,1:T(8,128)(2,1)S(1)} %collective-permute-done.10), channel_id=1, source_target_pairs={{0,4},{4,8},{8,12},{12,16},{16,20},{20,24},{24,28},{1,5},{5,9},{9,... | collective-permute-start | bytes 24584 | tf_op jit(solution)/shard_map/ppermute | solution.py:15
  35.2 9.0 %collective-permute-start.2 = (bf16[128,1024]{1,0:T(8,128)(2,1)}, bf16[128,1024]{1,0:T(8,128)(2,1)}, u32[]{:S(2)}, u32[]{:S(2)}) collective-permute-start(bf16[128,1024]{1,0:T(8,128)(2,1)} %collective-permute-done.1), channel_id=1, source_target_pairs={{0,4},{4,8},{8,12},{12,16},{16,20},{20,24},{24,28},{1,5},{5,9},{9,... | collective-permute-start | bytes 786440 | tf_op jit(solution)/shard_map/ppermute | solution.py:15
  98.7 8.6 %copy-start.3 = (f32[4,128,2,2,128]{1,4,3,2,0:T(8,128)S(1)}, f32[4,128,2,2,128]{1,4,3,2,0:T(8,128)}, u32[]{:S(2)}) copy-start(f32[4,128,2,2,128]{1,4,3,2,0:T(8,128)} %get-tuple-element.63) | copy-start | bytes 3145732
  102.1 10.5 %collective-permute-start.12 = (f32[128,16]{0,1:T(8,128)S(1)}, f32[128,16]{0,1:T(8,128)S(1)}, u32[]{:S(2)}, u32[]{:S(2)}) collective-permute-start(f32[128,16]{0,1:T(8,128)S(1)} %get-tuple-element.147), channel_id=1, source_target_pairs={{4,0},{8,4},{12,8},{16,12},{20,16},{24,20},{28,24},{5,1},{9,5},{13... | collective-permute-start | bytes 24584 | tf_op jit(solution)/shard_map/ppermute | solution.py:15
  103.4 10.7 %collective-permute-start.13 = (f32[128,16]{0,1:T(8,128)S(1)}, f32[128,16]{0,1:T(8,128)S(1)}, u32[]{:S(2)}, u32[]{:S(2)}) collective-permute-start(f32[128,16]{0,1:T(8,128)S(1)} %get-tuple-element.149), channel_id=1, source_target_pairs={{8,0},{12,4},{16,8},{20,12},{24,16},{28,20},{9,1},{13,5},{17,9},{2... | collective-permute-start | bytes 24584 | tf_op jit(solution)/shard_map/ppermute | solution.py:15
  104.7 9.4 %collective-permute-start.14 = (f32[128,16]{0,1:T(8,128)S(1)}, f32[128,16]{0,1:T(8,128)S(1)}, u32[]{:S(2)}, u32[]{:S(2)}) collective-permute-start(f32[128,16]{0,1:T(8,128)S(1)} %get-tuple-element.148), channel_id=1, source_target_pairs={{12,0},{16,4},{20,8},{24,12},{28,16},{13,1},{17,5},{21,9},{25,13},... | collective-permute-start | bytes 24584 | tf_op jit(solution)/shard_map/ppermute | solution.py:15
  106.0 9.1 %collective-permute-start.6 = (f32[128,16]{0,1:T(8,128)S(1)}, f32[128,16]{0,1:T(8,128)S(1)}, u32[]{:S(2)}, u32[]{:S(2)}) collective-permute-start(f32[128,16]{0,1:T(8,128)S(1)} %get-tuple-element.150), channel_id=1, source_target_pairs={{4,0},{8,4},{12,8},{16,12},{20,16},{24,20},{28,24},{5,1},{9,5},{13... | collective-permute-start | bytes 24584 | tf_op jit(solution)/shard_map/ppermute | solution.py:15
  111.3 7.2 %collective-permute-start.7 = (f32[128,16]{0,1:T(8,128)S(1)}, f32[128,16]{0,1:T(8,128)S(1)}, u32[]{:S(2)}, u32[]{:S(2)}) collective-permute-start(f32[128,16]{0,1:T(8,128)S(1)} %get-tuple-element.152), channel_id=1, source_target_pairs={{8,0},{12,4},{16,8},{20,12},{24,16},{28,20},{9,1},{13,5},{17,9},{2... | collective-permute-start | bytes 24584 | tf_op jit(solution)/shard_map/ppermute | solution.py:15
  112.6 9.4 %copy-start.11 = (bf16[4,128,2,2,128]{1,4,3,2,0:T(8,128)(2,1)S(1)}, bf16[4,128,2,2,128]{1,4,3,2,0:T(8,128)(2,1)}, u32[]{:S(2)}) copy-start(bf16[4,128,2,2,128]{1,4,3,2,0:T(8,128)(2,1)} %get-tuple-element.62) | copy-start | bytes 1572868
  112.6 8.3 %collective-permute-start.8 = (f32[128,16]{0,1:T(8,128)S(1)}, f32[128,16]{0,1:T(8,128)S(1)}, u32[]{:S(2)}, u32[]{:S(2)}) collective-permute-start(f32[128,16]{0,1:T(8,128)S(1)} %get-tuple-element.151), channel_id=1, source_target_pairs={{12,0},{16,4},{20,8},{24,12},{28,16},{13,1},{17,5},{21,9},{25,13},... | collective-permute-start | bytes 24584 | tf_op jit(solution)/shard_map/ppermute | solution.py:15
  (25 other events, 81.0 us)
Sparse Core Ops, SparseCore 0:
  122.2 135.2 all-reduce.2
where the time goes:
time: 275 us; the launch traced here: 273 us
  waiting for transfers between devices  140 us (51%)
  matrix products  55.3 us (20%)
  starting transfers between devices  33.4 us (12%)
  local copies, waits for them, and re-layouts  18.8 us (7%)
  between operations  15.2 us (6%)
  other arithmetic  10.2 us (4%)
    psum x1, waiting for transfers between devices, shards(): lax.psum((grad_a_query, grad_b_query, grad_a_key, grad_b_key, grad_a_valu...  134 us
    ppermute x15, starting transfers between devices, shifted(): lax.ppermute(value, axis, [(source, source + steps) for source in range(l...  33.4 us
    unnamed x49, local copies, waits for them, and re-layouts  11.3 us
    dot_general x4, matrix products, attend(): jnp.einsum('grqk,qgrd->kgd', probs_low, d_out, preferred_element_type=jnp...  10 us
    dot_general x4, matrix products, attend(): jnp.einsum('grqk,qgrd->kgd', dscore, query, preferred_element_type=jnp.fl...  8.35 us
    dot_general x4, matrix products, attend(): jnp.einsum('grqk,kgd->qgrd', probs_low, values, preferred_element_type=jn...  6.73 us
    ppermute x15, waiting for transfers between devices, shifted(): lax.ppermute(value, axis, [(source, source + steps) for source in range(l...  5.89 us
    sub x4, matrix products, attend(): raw_weight = jnp.exp(scores - top_score)  5.62 us
  transfers between devices with their start and end apart: 16, of which 3 were waited for; matrix products, arithmetic and copies ran while one was open for 5% of the time, Pallas kernels for 0%

commit v1 on v0

--- a/solution.py
+++ b/solution.py
@@ -145,8 +145,10 @@
     grad_a_key = jnp.einsum("td,tr->dr", rows, u_key, preferred_element_type=jnp.float32)
     grad_a_value = jnp.einsum("td,tr->dr", rows, u_value, preferred_element_type=jnp.float32)
     totals = lax.psum(
-        (grad_a_query, grad_b_query, grad_a_key, grad_b_key, grad_a_value, grad_b_value),
-        ("seq", "dp"),
+        lax.psum(
+            (grad_a_query, grad_b_query, grad_a_key, grad_b_key, grad_a_value, grad_b_value), "dp"
+        ),
+        "seq",
     )
     return (attention[None], totals[0], totals[1], totals[2], totals[3], totals[4], totals[5])
 

time: 275 us -> 265 us (0.964)
  waiting for transfers between devices: 140 us -> 131 us
    psum x1, waiting for transfers between devices: 134 us -> 64.4 us  [shards(): lax.psum((grad_a_query, grad_b_query, grad_a_key, grad_b_key, grad_a_valu...]
    psum x0 -> x1, waiting for transfers between devices: none -> 60.8 us  [shards(): lax.psum(lax.psum((grad_a_query, grad_b_query, grad_a_key, grad_b_key, gr...]
  transfers between devices with their start and end apart: 16 -> 17, of which waited for: 3 -> 4; matrix products, arithmetic and copies ran while one was open for 5% -> 5% of each run, Pallas kernels for 0% -> 0%
where the time goes in v1:
time: 265 us; the launch traced here: 264 us
  waiting for transfers between devices  131 us (49%)
  matrix products  55.2 us (21%)
  starting transfers between devices  33.4 us (13%)
  local copies, waits for them, and re-layouts  18.8 us (7%)
  between operations  15.2 us (6%)
  other arithmetic  10.1 us (4%)
    psum x1, waiting for transfers between devices, shards(): lax.psum((grad_a_query, grad_b_query, grad_a_key, grad_b_key, grad_a_valu...  64.4 us
    psum x1, waiting for transfers between devices, shards(): lax.psum(lax.psum((grad_a_query, grad_b_query, grad_a_key, grad_b_key, gr...  60.8 us
    ppermute x15, starting transfers between devices, shifted(): lax.ppermute(value, axis, [(source, source + steps) for source in range(l...  33.3 us
    unnamed x49, local copies, waits for them, and re-layouts  11.3 us
    dot_general x4, matrix products, attend(): jnp.einsum('grqk,qgrd->kgd', probs_low, d_out, preferred_element_type=jnp...  10 us
    dot_general x4, matrix products, attend(): jnp.einsum('grqk,qgrd->kgd', dscore, query, preferred_element_type=jnp.fl...  8.3 us
    dot_general x4, matrix products, attend(): jnp.einsum('grqk,kgd->qgrd', probs_low, values, preferred_element_type=jn...  6.72 us
    ppermute x15, waiting for transfers between devices, shifted(): lax.ppermute(value, axis, [(source, source + steps) for source in range(l...  5.89 us
  transfers between devices with their start and end apart: 17, of which 4 were waited for; matrix products, arithmetic and copies ran while one was open for 5% of the time, Pallas kernels for 0%

profile of v1, /device:TPU:0, one launch (start us, length us, event | category | flops | bytes accessed | tf_op | source)
XLA Modules:
  0.0 264.1 jit_solution(5436133574997863134)
XLA Ops:
  10.4 3.1 %collective-permute-start.3 = (bf16[128,1024]{1,0:T(8,128)(2,1)S(1)}, bf16[128,1024]{1,0:T(8,128)(2,1)}, u32[]{:S(2)}, u32[]{:S(2)}) collective-permute-start(bf16[128,1024]{1,0:T(8,128)(2,1)S(1)} %fusion.78), channel_id=1, source_target_pairs={{0,4},{4,8},{8,12},{12,16},{16,20},{20,24},{24,28},{1,5},{5,9},{9,... | collective-permute-start | bytes 786440 | tf_op jit(solution)/shard_map/ppermute | solution.py:15
  13.8 4.5 %collective-permute-start = (bf16[128,1024]{1,0:T(8,128)(2,1)S(1)}, bf16[128,1024]{1,0:T(8,128)(2,1)}, u32[]{:S(2)}, u32[]{:S(2)}) collective-permute-start(bf16[128,1024]{1,0:T(8,128)(2,1)S(1)} %fusion.77), channel_id=1, source_target_pairs={{0,4},{4,8},{8,12},{12,16},{16,20},{20,24},{24,28},{1,5},{5,9},{9,... | collective-permute-start | bytes 786440 | tf_op jit(solution)/shard_map/ppermute | solution.py:15
  18.9 1.9 collective-permute-start.9
  22.1 2.9 %collective-permute-start.4 = (bf16[128,1024]{1,0:T(8,128)(2,1)}, bf16[128,1024]{1,0:T(8,128)(2,1)S(1)}, u32[]{:S(2)}, u32[]{:S(2)}) collective-permute-start(bf16[128,1024]{1,0:T(8,128)(2,1)} %collective-permute-done.3), channel_id=1, source_target_pairs={{0,4},{4,8},{8,12},{12,16},{16,20},{20,24},{24,28},{1,5},{5,9},{9,... | collective-permute-start | bytes 786440 | tf_op jit(solution)/shard_map/ppermute | solution.py:15
  25.0 2.6 collective-permute-start.1
  28.5 2.8 %collective-permute-start.10 = (bf16[128,32]{0,1:T(8,128)(2,1)}, bf16[128,32]{0,1:T(8,128)(2,1)S(1)}, u32[]{:S(2)}, u32[]{:S(2)}) collective-permute-start(bf16[128,32]{0,1:T(8,128)(2,1)} %collective-permute-done.9), channel_id=1, source_target_pairs={{0,4},{4,8},{8,12},{12,16},{16,20},{20,24},{24,28},{1,5},{5,9},{9,... | collective-permute-start | bytes 24584 | tf_op jit(solution)/shard_map/ppermute | solution.py:15
  31.3 1.9 collective-permute-start.5
  33.3 1.9 collective-permute-start.11
  35.2 4.0 %collective-permute-start.2 = (bf16[128,1024]{1,0:T(8,128)(2,1)}, bf16[128,1024]{1,0:T(8,128)(2,1)}, u32[]{:S(2)}, u32[]{:S(2)}) collective-permute-start(bf16[128,1024]{1,0:T(8,128)(2,1)} %collective-permute-done.1), channel_id=1, source_target_pairs={{0,4},{4,8},{8,12},{12,16},{16,20},{20,24},{24,28},{1,5},{5,9},{9,... | collective-permute-start | bytes 786440 | tf_op jit(solution)/shard_map/ppermute | solution.py:15
  47.6 47.7 %while.17 = (s32[]{:T(128)}, bf16[4,128,2,2,128]{1,4,3,2,0:T(8,128)(2,1)}, f32[4,128,2,2,128]{1,4,3,2,0:T(8,128)}, f32[4,512,2,128]{1,3,2,0:T(8,128)}, f32[4,512...) while((s32[]{:T(128)}, ...), condition=%wide.region_4.5_spmd.clone, body=%wide.region_0.4_spmd.clone.sunk | while | flops 543098880 | bytes 17327832 | solution.py:111
  51.5 2.1 fusion.172
  54.5 2.5 fusion.173
  63.4 2.1 fusion.172
  66.5 2.5 fusion.173
  75.3 2.1 fusion.172
  78.4 2.5 fusion.173
  87.2 2.1 fusion.172
  90.3 2.5 fusion.173
  95.3 2.5 fusion.118
  109.3 1.9 fusion.104
  114.9 3.5 %collective-permute-done.7 = f32[128,16]{0,1:T(8,128)S(1)} collective-permute-done((f32[128,16]{0,1:T(8,128)S(1)}, f32[128,16]{0,1:T(8,128)S(1)}, u32[]{:S(2)}, u32[]{:S(2)}) %collective-permute-start.7) | collective-permute-done | bytes 8224 | tf_op jit(solution)/shard_map/ppermute | solution.py:15
  118.4 2.4 collective-permute-done.8
  121.9 64.4 %all-reduce.7.cloned.1.call-done = (f32[5376,16]{0,1:T(8,128)}, f32[16,2048]{1,0:T(8,128)}, f32[5376,16]{0,1:T(8,128)}, f32[16,1024]{1,0:T(8,128)}, f32[5376,16]{0,1:T(8,128)}, /*index=5*/f32[16,1024]{1,0:T(8,128)}) async-done(((f32[5376,16]{0,1:T(8,128)}, f32[16,2048]{1,0:T(8,128)}, f32[5376,16]{0,1:T(8,128)}, f32[16,1024]{1,0:T(8,128)}, f32[5376,16]{0,1:T(8,128)}, /*index=5*/f32[16,1024]{1,0:T(8,128)}), ...) | async-done | bytes 1294352 | tf_op jit(solution)/shard_map/psum | solution.py:148
  187.5 60.8 %all-reduce.5.cloned.1.call-done = (f32[5376,16]{0,1:T(8,128)}, f32[16,2048]{1,0:T(8,128)}, f32[5376,16]{0,1:T(8,128)}, f32[16,1024]{1,0:T(8,128)}, f32[5376,16]{0,1:T(8,128)}, /*index=5*/f32[16,1024]{1,0:T(8,128)}) async-done(((f32[5376,16]{0,1:T(8,128)}, f32[16,2048]{1,0:T(8,128)}, f32[5376,16]{0,1:T(8,128)}, f32[16,1024]{1,0:T(8,128)}, f32[5376,16]{0,1:T(8,128)}, /*index=5*/f32[16,1024]{1,0:T(8,128)}), ...) | async-done | bytes 1294352 | tf_op jit(solution)/shard_map/psum | solution.py:147
  (153 shorter events, 69.3 us)
Async XLA Ops:
  7.2 14.2 %copy-start.7 = (bf16[1,128,2048]{2,1,0:T(8,128)(2,1)S(1)}, bf16[1,128,2048]{2,1,0:T(8,128)(2,1)}, u32[]{:S(2)}) copy-start(bf16[1,128,2048]{2,1,0:T(8,128)(2,1)} %param.18) | copy-start | bytes 1572868
  7.2 14.5 %copy-start.8 = (bf16[1,128,2048]{2,1,0:T(8,128)(2,1)S(1)}, bf16[1,128,2048]{2,1,0:T(8,128)(2,1)}, u32[]{:S(2)}) copy-start(bf16[1,128,2048]{2,1,0:T(8,128)(2,1)} %param.15) | copy-start | bytes 1572868
  7.2 14.5 %copy-start.12 = (bf16[16,2048]{1,0:T(8,128)(2,1)S(1)}, bf16[16,2048]{1,0:T(8,128)(2,1)}, u32[]{:S(2)}) copy-start(bf16[16,2048]{1,0:T(8,128)(2,1)} %param.21) | copy-start | bytes 196612
  7.2 179.0 %all-reduce.7.cloned.1.call-start = ((), (), s32[]{:S(2)}) async-start(), calls=%async_computation.1 | async-start | bytes 2588672 | tf_op jit(solution)/shard_map/psum | solution.py:148
  10.2 18.3 %copy-start.21 = (bf16[128,48]{0,1:T(8,128)(2,1)}, bf16[128,48]{0,1:T(8,128)(2,1)S(1)}, u32[]{:S(2)}) copy-start(bf16[128,48]{0,1:T(8,128)(2,1)S(1)} %fusion.82) | copy-start | bytes 36868
  10.4 11.6 %collective-permute-start.3 = (bf16[128,1024]{1,0:T(8,128)(2,1)S(1)}, bf16[128,1024]{1,0:T(8,128)(2,1)}, u32[]{:S(2)}, u32[]{:S(2)}) collective-permute-start(bf16[128,1024]{1,0:T(8,128)(2,1)S(1)} %fusion.78), channel_id=1, source_target_pairs={{0,4},{4,8},{8,12},{12,16},{16,20},{20,24},{24,28},{1,5},{5,9},{9,... | collective-permute-start | bytes 786440 | tf_op jit(solution)/shard_map/ppermute | solution.py:15
  13.8 26.3 %copy-start.5 = (bf16[128,1024]{1,0:T(8,128)(2,1)}, bf16[128,1024]{1,0:T(8,128)(2,1)S(1)}, u32[]{:S(2)}) copy-start(bf16[128,1024]{1,0:T(8,128)(2,1)S(1)} %fusion.77) | copy-start | bytes 786436
  13.8 11.2 %collective-permute-start = (bf16[128,1024]{1,0:T(8,128)(2,1)S(1)}, bf16[128,1024]{1,0:T(8,128)(2,1)}, u32[]{:S(2)}, u32[]{:S(2)}) collective-permute-start(bf16[128,1024]{1,0:T(8,128)(2,1)S(1)} %fusion.77), channel_id=1, source_target_pairs={{0,4},{4,8},{8,12},{12,16},{16,20},{20,24},{24,28},{1,5},{5,9},{9,... | collective-permute-start | bytes 786440 | tf_op jit(solution)/shard_map/ppermute | solution.py:15
  18.9 9.6 %collective-permute-start.9 = (bf16[128,32]{0,1:T(8,128)(2,1)}, bf16[128,32]{0,1:T(8,128)(2,1)}, u32[]{:S(2)}, u32[]{:S(2)}) collective-permute-start(bf16[128,32]{0,1:T(8,128)(2,1)} %slice.65), channel_id=1, source_target_pairs={{0,4},{4,8},{8,12},{12,16},{16,20},{20,24},{24,28},{1,5},{5,9},{9,... | collective-permute-start | bytes 24584 | tf_op jit(solution)/shard_map/ppermute | solution.py:15
  22.1 9.2 %collective-permute-start.4 = (bf16[128,1024]{1,0:T(8,128)(2,1)}, bf16[128,1024]{1,0:T(8,128)(2,1)S(1)}, u32[]{:S(2)}, u32[]{:S(2)}) collective-permute-start(bf16[128,1024]{1,0:T(8,128)(2,1)} %collective-permute-done.3), channel_id=1, source_target_pairs={{0,4},{4,8},{8,12},{12,16},{16,20},{20,24},{24,28},{1,5},{5,9},{9,... | collective-permute-start | bytes 786440 | tf_op jit(solution)/shard_map/ppermute | solution.py:15
  25.0 10.2 %collective-permute-start.1 = (bf16[128,1024]{1,0:T(8,128)(2,1)}, bf16[128,1024]{1,0:T(8,128)(2,1)}, u32[]{:S(2)}, u32[]{:S(2)}) collective-permute-start(bf16[128,1024]{1,0:T(8,128)(2,1)} %collective-permute-done), channel_id=1, source_target_pairs={{0,4},{4,8},{8,12},{12,16},{16,20},{20,24},{24,28},{1,5},{5,9},{9,... | collective-permute-start | bytes 786440 | tf_op jit(solution)/shard_map/ppermute | solution.py:15
  28.5 4.8 %collective-permute-start.10 = (bf16[128,32]{0,1:T(8,128)(2,1)}, bf16[128,32]{0,1:T(8,128)(2,1)S(1)}, u32[]{:S(2)}, u32[]{:S(2)}) collective-permute-start(bf16[128,32]{0,1:T(8,128)(2,1)} %collective-permute-done.9), channel_id=1, source_target_pairs={{0,4},{4,8},{8,12},{12,16},{16,20},{20,24},{24,28},{1,5},{5,9},{9,... | collective-permute-start | bytes 24584 | tf_op jit(solution)/shard_map/ppermute | solution.py:15
  31.3 11.0 %collective-permute-start.5 = (bf16[128,1024]{1,0:T(8,128)(2,1)S(1)}, bf16[128,1024]{1,0:T(8,128)(2,1)S(1)}, u32[]{:S(2)}, u32[]{:S(2)}) collective-permute-start(bf16[128,1024]{1,0:T(8,128)(2,1)S(1)} %collective-permute-done.4), channel_id=1, source_target_pairs={{0,4},{4,8},{8,12},{12,16},{16,20},{20,24},{24,28},{1,5},{5,9},{9,... | collective-permute-start | bytes 786440 | tf_op jit(solution)/shard_map/ppermute | solution.py:15
  33.3 7.7 %collective-permute-start.11 = (bf16[128,32]{0,1:T(8,128)(2,1)S(1)}, bf16[128,32]{0,1:T(8,128)(2,1)S(1)}, u32[]{:S(2)}, u32[]{:S(2)}) collective-permute-start(bf16[128,32]{0,1:T(8,128)(2,1)S(1)} %collective-permute-done.10), channel_id=1, source_target_pairs={{0,4},{4,8},{8,12},{12,16},{16,20},{20,24},{24,28},{1,5},{5,9},{9,... | collective-permute-start | bytes 24584 | tf_op jit(solution)/shard_map/ppermute | solution.py:15
  35.2 9.1 %collective-permute-start.2 = (bf16[128,1024]{1,0:T(8,128)(2,1)}, bf16[128,1024]{1,0:T(8,128)(2,1)}, u32[]{:S(2)}, u32[]{:S(2)}) collective-permute-start(bf16[128,1024]{1,0:T(8,128)(2,1)} %collective-permute-done.1), channel_id=1, source_target_pairs={{0,4},{4,8},{8,12},{12,16},{16,20},{20,24},{24,28},{1,5},{5,9},{9,... | collective-permute-start | bytes 786440 | tf_op jit(solution)/shard_map/ppermute | solution.py:15
  102.0 10.5 %collective-permute-start.12 = (f32[128,16]{0,1:T(8,128)S(1)}, f32[128,16]{0,1:T(8,128)S(1)}, u32[]{:S(2)}, u32[]{:S(2)}) collective-permute-start(f32[128,16]{0,1:T(8,128)S(1)} %get-tuple-element.153), channel_id=1, source_target_pairs={{4,0},{8,4},{12,8},{16,12},{20,16},{24,20},{28,24},{5,1},{9,5},{13... | collective-permute-start | bytes 24584 | tf_op jit(solution)/shard_map/ppermute | solution.py:15
  103.3 10.5 %collective-permute-start.13 = (f32[128,16]{0,1:T(8,128)S(1)}, f32[128,16]{0,1:T(8,128)S(1)}, u32[]{:S(2)}, u32[]{:S(2)}) collective-permute-start(f32[128,16]{0,1:T(8,128)S(1)} %get-tuple-element.155), channel_id=1, source_target_pairs={{8,0},{12,4},{16,8},{20,12},{24,16},{28,20},{9,1},{13,5},{17,9},{2... | collective-permute-start | bytes 24584 | tf_op jit(solution)/shard_map/ppermute | solution.py:15
  104.6 9.3 %collective-permute-start.14 = (f32[128,16]{0,1:T(8,128)S(1)}, f32[128,16]{0,1:T(8,128)S(1)}, u32[]{:S(2)}, u32[]{:S(2)}) collective-permute-start(f32[128,16]{0,1:T(8,128)S(1)} %get-tuple-element.154), channel_id=1, source_target_pairs={{12,0},{16,4},{20,8},{24,12},{28,16},{13,1},{17,5},{21,9},{25,13},... | collective-permute-start | bytes 24584 | tf_op jit(solution)/shard_map/ppermute | solution.py:15
  105.9 9.0 %collective-permute-start.6 = (f32[128,16]{0,1:T(8,128)S(1)}, f32[128,16]{0,1:T(8,128)S(1)}, u32[]{:S(2)}, u32[]{:S(2)}) collective-permute-start(f32[128,16]{0,1:T(8,128)S(1)} %get-tuple-element.156), channel_id=1, source_target_pairs={{4,0},{8,4},{12,8},{16,12},{20,16},{24,20},{28,24},{5,1},{9,5},{13... | collective-permute-start | bytes 24584 | tf_op jit(solution)/shard_map/ppermute | solution.py:15
  111.3 7.1 %collective-permute-start.7 = (f32[128,16]{0,1:T(8,128)S(1)}, f32[128,16]{0,1:T(8,128)S(1)}, u32[]{:S(2)}, u32[]{:S(2)}) collective-permute-start(f32[128,16]{0,1:T(8,128)S(1)} %get-tuple-element.158), channel_id=1, source_target_pairs={{8,0},{12,4},{16,8},{20,12},{24,16},{28,20},{9,1},{13,5},{17,9},{2... | collective-permute-start | bytes 24584 | tf_op jit(solution)/shard_map/ppermute | solution.py:15
  112.6 8.2 %collective-permute-start.8 = (f32[128,16]{0,1:T(8,128)S(1)}, f32[128,16]{0,1:T(8,128)S(1)}, u32[]{:S(2)}, u32[]{:S(2)}) collective-permute-start(f32[128,16]{0,1:T(8,128)S(1)} %get-tuple-element.157), channel_id=1, source_target_pairs={{12,0},{16,4},{20,8},{24,12},{28,16},{13,1},{17,5},{21,9},{25,13},... | collective-permute-start | bytes 24584 | tf_op jit(solution)/shard_map/ppermute | solution.py:15
  114.9 71.4 %copy-start.11 = (bf16[4,128,2,2,128]{1,4,3,2,0:T(8,128)(2,1)S(1)}, bf16[4,128,2,2,128]{1,4,3,2,0:T(8,128)(2,1)}, u32[]{:S(2)}) copy-start(bf16[4,128,2,2,128]{1,4,3,2,0:T(8,128)(2,1)} %get-tuple-element.62) | copy-start | bytes 1572868
  121.8 64.7 %copy-start.23 = (pred[128]{0:T(512)(128)(4,1)S(1)}, pred[128]{0:T(512)(128)(4,1)}, u32[]{:S(2)}) copy-start(pred[128]{0:T(512)(128)(4,1)} %copy-done.22) | copy-start | bytes 388
  121.8 126.5 %all-reduce.5.cloned.1.call-start = ((), (), s32[]{:S(2)}) async-start(), calls=%async_computation | async-start | bytes 2588672 | tf_op jit(solution)/shard_map/psum | solution.py:147
  (26 other events, 94.1 us)
Sparse Core Ops, SparseCore 0:
  122.0 64.2 all-reduce.6
  190.2 58.0 all-reduce.4
